TPU v7x, 32 devices: a whole 2x2x4 slice. The times are simulated.
32 devices in a mesh: groups: 2 (over x), fsdp: 16 (over z, y, core).
Axes of the slice: x: 2, y: 2, z: 4, core: 2. Of those that a mesh axis runs over, the one named last changes fastest.
Arguments:
- qkv: bfloat16 [8192, 9600], P(('groups', 'fsdp')), parts along dimension 0, may hold values from -22.5 to 22.5
- patches: bfloat16 [8192, 3200], P(('groups', 'fsdp')), parts along dimension 0, may hold values from -40 to 40
- frame_starts: int32 [2048], P(('groups', 'fsdp')), parts along dimension 0, may hold values from 0 to 1, as said below
- out_weight: bfloat16 [3200, 3200], P(None, 'fsdp'), may hold values from -0.109375 to 0.109375
- layer_scale: float32 [3200], replicated, may hold values from 0.5 to 5
- norm_gain: float32 [12800], replicated, may hold values from 0.1 to 1.9
- norm_bias: float32 [12800], replicated, may hold values from -3 to 3
- owners: int32 [2048, 1], P(('groups', 'fsdp')), parts along dimension 0, may hold values from 0 to 15; in each aligned block of 64 rows (0 to 63, 64 to 127, ...) at most 8 rows name the same one
Outputs:
- owned: bfloat16 [4096, 12800], P(('groups', 'fsdp')), parts along dimension 0
There are 2 independent parts, one for each index of `groups`. A program takes and returns all parts, laid end to end along the dimension named above; an argument that names none is the same for every part. Nothing has to cross between parts.
Inputs may be any that keep to these rules, and one draw needn't show every extreme that they name: `frame_starts`: 1 at the first merged row of each device's block of 64, so frames never cross a block. `owners`: in each aligned block of 64 merged rows (one device's) no owner is named more than 8 times.
All inputs are finite; a program needn't handle non-finite values.
Results may differ from a plain program's by a relative error of at most 0.0095.
Values may be sent and summed in bfloat16 or wider, within the bound.
A program may use at most 128 MiB of HBM per device.

v0:
```python
import math

import jax
import jax.numpy as jnp
from jax import lax
from jax.sharding import PartitionSpec as P

HEADS = 25


def layer_norm(merged, norm_gain, norm_bias):
    values = merged.astype(jnp.float32)
    centre = jnp.mean(values, axis=-1, keepdims=True)
    centered = values - centre
    variance = jnp.mean(centered * centered, axis=-1, keepdims=True)
    return centered * lax.rsqrt(variance + 1e-05) * norm_gain + norm_bias


def local(qkv, patches, frame_starts, out_weight, layer_scale, norm_gain, norm_bias, owners):
    tok_rows = qkv.shape[0]
    model_width = patches.shape[1]
    head_size = model_width // HEADS
    frames = jnp.repeat(jnp.cumsum(frame_starts), 4)
    queries = qkv[:, :model_width].reshape(tok_rows, HEADS, head_size)
    key_heads = qkv[:, model_width : 2 * model_width].reshape(tok_rows, HEADS, head_size)
    value_heads = qkv[:, 2 * model_width :].reshape(tok_rows, HEADS, head_size)
    scores = jnp.einsum("qhd,khd->hqk", queries, key_heads, preferred_element_type=jnp.float32)
    scores = scores * (1.0 / math.sqrt(head_size))
    same_frame = frames[:, None] == frames[None, :]
    scores = jnp.where(same_frame[None], scores, -1e30)
    row_max = jnp.max(scores, axis=-1, keepdims=True)
    exps = jnp.exp(scores - row_max)
    weights = (exps / jnp.sum(exps, axis=-1, keepdims=True)).astype(jnp.bfloat16)
    context = jnp.einsum("hqk,khd->qhd", weights, value_heads, preferred_element_type=jnp.float32)
    context = context.reshape(tok_rows, model_width).astype(jnp.bfloat16)
    full_weight = lax.all_gather(out_weight, "fsdp", axis=1, tiled=True)
    projected = jnp.dot(context, full_weight, preferred_element_type=jnp.float32)
    layer_out = (patches.astype(jnp.float32) + layer_scale * projected).astype(jnp.bfloat16)
    quad_rows = tok_rows // 4
    merged = layer_out.reshape(quad_rows, 4 * model_width)
    devices = lax.axis_size("fsdp")
    capacity = max(2, 2 * quad_rows // devices)
    owner_ids = owners[:, 0]
    one_hot = (owner_ids[:, None] == jnp.arange(devices, dtype=jnp.int32)[None, :]).astype(
        jnp.int32
    )
    earlier = jnp.cumsum(one_hot, axis=0) - one_hot
    ranking = jnp.sum(earlier * one_hot, axis=1)
    target = owner_ids * capacity + ranking
    normed = layer_norm(merged, norm_gain, norm_bias).astype(jnp.bfloat16)
    buffer = jnp.zeros((devices * capacity, 4 * model_width), jnp.bfloat16).at[target].set(normed)
    received = lax.all_to_all(
        buffer.reshape(devices, capacity, 4 * model_width),
        "fsdp",
        split_axis=0,
        concat_axis=0,
        tiled=True,
    )
    return received.reshape(devices * capacity, 4 * model_width)


def solution(mesh):
    return jax.shard_map(
        local,
        mesh=mesh,
        in_specs=(
            P(("groups", "fsdp"), None),
            P(("groups", "fsdp"), None),
            P(("groups", "fsdp")),
            P(None, "fsdp"),
            P(),
            P(),
            P(),
            P(("groups", "fsdp"), None),
        ),
        out_specs=P(("groups", "fsdp"), None),
        check_vma=False,
    )
```

profile of v0, /device:TPU:13, one launch (start us, length us, event | category | flops | bytes accessed | tf_op | source)
XLA Modules:
  0.0 226.5 jit_solution(4748388122903106867)
XLA Ops:
  6.5 0.7 all-gather.2.cloned.1.call-update
  7.3 3.9 %fusion.18 = (bf16[256,3200]{1,0:T(8,128)(2,1)S(1)}, bf16[256,3200]{1,0:T(8,128)(2,1)}, bf16[256,3200]{1,0:T(8,128)(2,1)S(1)}) fusion(bf16[256,9600]{1,0:T(8,128)(2,1)} %param.8), kind=kLoop, calls=%fused_computation.31 | loop fusion | bytes 9830400 | tf_op jit(solution)/shard_map/slice | solution.py:25
  11.2 3.7 %copy.22 = bf16[256,3200]{0,1:T(8,128)(2,1)} copy(bf16[256,3200]{1,0:T(8,128)(2,1)} %get-tuple-element.6) | data formatting | bytes 3276800
  14.9 2.2 copy.23
  17.3 0.1 reduce.4
  17.5 0.1 eq.38
  17.6 2.2 copy.17
  20.0 0.2 select_reduce_fusion
  20.2 0.1 broadcast_compare_fusion
  20.4 6.6 %fusion.19 = (f32[25,256]{1,0:T(8,128)S(1)}, f32[25,256,256]{1,2,0:T(8,128)}) fusion(pred[256,256]{0,1:T(8,128)(4,1)S(1)} %broadcast_compare_fusion, bf16[256,25,128]{0,2,1:T(8,128)(2,1)S(1)} %bitcast.25, bf16[256,25,128]{0,2,1:T(8,128)(2,1)} %bitcast.26), kind=kOutput, calls=%fused_computation.32 | convolution fusion | flops 425984256 | bytes 9921536 | tf_op jit(solution)/shard_map/sub | solution.py:32
  27.0 4.8 %fusion.9 = bf16[25,256,128]{1,2,0:T(8,128)(2,1)} fusion(bf16[256,25,128]{0,2,1:T(8,128)(2,1)S(1)} %bitcast.27, f32[25,256,256]{1,2,0:T(8,128)} %get-tuple-element.9, f32[25,256]{1,0:T(8,128)S(1)} %get-tuple-element.8), kind=kOutput, calls=%fused_computation.16 | convolution fusion | flops 423526400 | bytes 9856000 | tf_op jit(solution)/shard_map/hqk,khd->qhd/dot_general | solution.py:34
  31.8 85.1 %all-gather.2.cloned.1.call-done = bf16[3200,3200]{0,1:T(8,128)(2,1)} async-done(((bf16[3200,200]{0,1:T(8,128)(2,1)}), bf16[3200,3200]{0,1:T(8,128)(2,1)}) %all-gather.2.cloned.1.call-update) | async-done | bytes 20480016 | tf_op jit(solution)/shard_map/all_gather | solution.py:36
  116.9 11.7 %fusion.20 = (f32[256]{0:T(256)S(1)}, f32[256,3200]{1,0:T(8,128)S(1)}) fusion(bf16[256,3200]{0,1:T(8,128)(2,1)} %bitcast.31, bf16[3200,3200]{0,1:T(8,128)(2,1)} %all-gather.2.cloned.1.call-done, f32[3200]{0:T(1024)S(1)} %copy-done.6, bf16[256,3200]{1,0:T(8,128)(2,1)} %param.9), kind=kOutput, calls=%fused_computation.33 | convolution fusion | flops 5247795200 | bytes 27047424 | tf_op jit(solution)/shard_map/dot_general | solution.py:37
  128.6 0.1 reduce_sum.56
  128.7 0.1 reduce_sum.57
  128.9 0.1 sub.34
  129.0 2.0 reshape.107
  131.0 0.5 multiply_reduce_fusion
  131.5 0.1 reduce_sum.59
  131.6 0.1 reduce_sum.60
  131.8 3.7 %add_convert_fusion = bf16[64,12800]{1,0:T(8,128)(2,1)} fusion(f32[64,12800]{1,0:T(8,128)} %reshape.107, f32[12800]{0:T(1024)S(1)} %copy-done.2, f32[12800]{0:T(1024)S(1)} %copy-done.3, f32[64]{0:T(128)S(1)} %add_rsqrt_fusion, f32[64]{0:T(128)S(1)} %broadcast_multiply_fusion), kind=kLoop, calls=%fused_computation.10 | loop fusion | flops 4096000 | bytes 5018112 | tf_op jit(solution)/shard_map/convert_element_type | solution.py:50
  135.5 4.7 %scatter_custom_fusion = bf16[128,12800]{1,0:T(8,128)(2,1)S(1)} fusion(s32[64]{0:T(128)S(1)} %fusion.15, bf16[64,12800]{1,0:T(8,128)(2,1)} %add_convert_fusion, bf16[]{:T(256)} %constant.10.clone.1), kind=kCustom, calls=%fused_computation.17 | custom fusion | bytes 3277312 | tf_op jit(solution)/shard_map/scatter | solution.py:51
  140.3 77.6 %all_to_all.5 = bf16[16,8,12800]{2,1,0:T(8,128)(2,1)S(1)} all-to-all(bf16[16,8,12800]{2,1,0:T(8,128)(2,1)S(1)} %bitcast.23), channel_id=1, replica_groups=mesh['groups'=2,'fsdp'=16] {'fsdp'}, dimensions={0} | all-to-all | bytes 6553600 | tf_op jit(solution)/shard_map/all_to_all | solution.py:52
  217.9 1.7 copy.25
  (24 shorter events, 0.7 us)
Async XLA Ops:
  6.5 110.4 %all-gather.2.cloned.1.call-start = ((), (), s32[]{:S(2)}) async-start(), calls=%async_computation.1 | async-start | bytes 21760000 | tf_op jit(solution)/shard_map/all_gather | solution.py:36
  11.2 5.9 %copy-start.5 = (s32[64]{0:T(128)S(1)}, s32[64]{0:T(128)}, u32[]{:S(2)}) copy-start(s32[64]{0:T(128)} %param.10) | copy-start | bytes 772
  14.9 5.0 %copy-start.4 = (s32[64,1]{0,1:T(1,128)S(1)}, s32[64,1]{0,1:T(1,128)}, u32[]{:S(2)}) copy-start(s32[64,1]{0,1:T(1,128)} %param.15) | copy-start | bytes 772
  17.1 3.2 %copy-start = (bf16[256,3200]{0,1:T(8,128)(2,1)S(1)}, bf16[256,3200]{0,1:T(8,128)(2,1)}, u32[]{:S(2)}) copy-start(bf16[256,3200]{0,1:T(8,128)(2,1)} %copy.22) | copy-start | bytes 4915204
  20.4 6.6 %copy-start.1 = (bf16[256,3200]{0,1:T(8,128)(2,1)S(1)}, bf16[256,3200]{0,1:T(8,128)(2,1)}, u32[]{:S(2)}) copy-start(bf16[256,3200]{0,1:T(8,128)(2,1)} %copy.17) | copy-start | bytes 4915204
  27.0 90.0 %copy-start.6 = (f32[3200]{0:T(1024)S(1)}, f32[3200]{0:T(1024)}, u32[]{:S(2)}) copy-start(f32[3200]{0:T(1024)} %param.12) | copy-start | bytes 38404
  131.0 0.8 copy-start.2
  131.0 0.8 copy-start.3
Sparse Core Ops, SparseCore 0:
  9.0 107.8 all-gather.1
where the time goes:
time: 229 us; the launch traced here: 226 us
  waiting for transfers between devices  85.9 us (38%)
  blocking collectives  77.6 us (34%)
  matrix products  23.1 us (10%)
  local copies, waits for them, and re-layouts  21.4 us (9%)
  between operations  13.5 us (6%)
  other arithmetic  5.06 us (2%)
    all_gather x1, waiting for transfers between devices, local(): full_weight = lax.all_gather(out_weight, 'fsdp', axis=1, tiled=True)  85.1 us
    all_to_all x1, blocking collectives, local(): lax.all_to_all(buffer.reshape(devices, capacity, 4 * model_width), 'fsdp'...  77.6 us
    dot_general x1, matrix products, local(): jnp.dot(context, full_weight, preferred_element_type=jnp.float32)  11.7 us
    unnamed x17, local copies, waits for them, and re-layouts  7.79 us
    sub x1, matrix products, local(): exps = jnp.exp(scores - row_max)  6.58 us
    dot_general x1, matrix products, local(): jnp.einsum('hqk,khd->qhd', weights, value_heads, preferred_element_type=j...  4.8 us
    scatter x1, local copies, waits for them, and re-layouts, local(): jnp.zeros((devices * capacity, 4 * model_width), jnp.bfloat16).at[target]  4.74 us
  transfers between devices with their start and end apart: 1, of which 1 were waited for; matrix products, arithmetic and copies ran while one was open for 11% of the time, Pallas kernels for 0%

commit v1 on v0

v1 whole, which is shorter than its diff:
```python
import functools
import math

import jax
import jax.numpy as jnp
from jax import lax
from jax.experimental import pallas as pl
from jax.experimental.pallas import tpu as pltpu
from jax.sharding import PartitionSpec as P

HEADS = 25
MESH = pl.DeviceIdType.MESH
F32 = jnp.float32
BF16 = jnp.bfloat16


def dot_nt(a, b):
    return lax.dot_general(a, b, (((1,), (1,)), ((), ())), preferred_element_type=F32)


def kernel(
    n,
    cols,
    part,
    qkv,
    patches,
    starts_row,
    starts_col,
    w_own,
    scale,
    gain,
    bias,
    owners_row,
    owners_col,
    out,
    w_all,
    ctx,
    acc,
    layer_out,
    merged,
    slots,
    ring_send,
    ring_recv,
    swap_send,
    swap_recv,
    core_send,
    core_recv,
    core_swap_send,
    core_swap_recv,
    own_send,
    own_recv,
    out_send,
    out_recv,
    local_sem,
):
    tok, width = patches.shape
    head = width // HEADS
    quads = tok // 4
    cap = out.shape[1]
    padded = w_own.shape[0]
    chips = n // 2
    g = lax.axis_index("groups")
    f = lax.axis_index("fsdp")
    parity = lax.rem(g, 2)
    partner = g + 1 - 2 * parity
    core = lax.rem(f, 2)
    chip = f // 2
    sibling = f + 1 - 2 * core
    place = jnp.where(lax.rem(chip, 2) == 0, chip // 2, chips - 1 - chip // 2)
    sign = 1 - 2 * core
    steps = (chips // 2, chips - 1 - chips // 2)

    def chip_at(p):
        p = lax.rem(p + 2 * chips, chips)
        return jnp.where(p < chips // 2, 2 * p, 2 * (chips - 1 - p) + 1)

    def way(side):
        return sign if side == 0 else -sign

    def ring_shard(side, s):
        return chip_at(place - way(side) * s) * 2 + core

    def core_shard(side, s):
        return chip_at(place + way(side) * s) * 2 + (1 - core)

    ring_rows = pl.ds(pl.multiple_of(parity * part, 16), padded - part)
    mine_rows = pl.ds(pl.multiple_of(parity * (padded - part), 16), part)
    theirs_rows = pl.ds(pl.multiple_of((1 - parity) * (padded - part), 16), part)

    def remote(src, dst, send, recv, device):
        return pltpu.make_async_remote_copy(
            src_ref=src, dst_ref=dst, send_sem=send, recv_sem=recv, device_id=device, device_id_type=MESH
        )

    def ring_copy(side, s):
        ref = w_all.at[ring_shard(side, s), ring_rows]
        to = chip_at(place + way(side)) * 2 + core
        return remote(ref, ref, ring_send.at[side, s], ring_recv.at[side, s], (g, to))

    def ring_arrival(side, s):
        ref = w_all.at[ring_shard(side, s + 1), ring_rows]
        return remote(ref, ref, ring_send.at[side, s], ring_recv.at[side, s], (g, sibling))

    def swap_copy(side, s):
        ref = w_all.at[ring_shard(side, s + 1), mine_rows]
        return remote(ref, ref, swap_send.at[side, s], swap_recv.at[side, s], (partner, f))

    def swap_arrival(side, s):
        ref = w_all.at[ring_shard(side, s + 1), theirs_rows]
        return remote(ref, ref, swap_send.at[side, s], swap_recv.at[side, s], (partner, f))

    def core_copy(side, s):
        ref = w_all.at[ring_shard(side, s + 1), ring_rows]
        return remote(ref, ref, core_send.at[side, s], core_recv.at[side, s], (g, sibling))

    def core_arrival(side, s):
        ref = w_all.at[core_shard(side, s + 1), ring_rows]
        return remote(ref, ref, core_send.at[side, s], core_recv.at[side, s], (g, sibling))

    def core_swap_copy(side, s):
        ref = w_all.at[ring_shard(side, s + 1), theirs_rows]
        return remote(ref, ref, core_swap_send.at[side, s], core_swap_recv.at[side, s], (g, sibling))

    def core_swap_arrival(side, s):
        ref = w_all.at[core_shard(side, s + 1), theirs_rows]
        return remote(ref, ref, core_swap_send.at[side, s], core_swap_recv.at[side, s], (g, sibling))

    def out_copy(d):
        to = lax.rem(f + d, n)
        return remote(slots.at[to], out.at[f], out_send.at[d], out_recv.at[d], (g, to))

    def out_arrival(d):
        frm = lax.rem(f + n - d, n)
        return remote(slots.at[frm], out.at[frm], out_send.at[d], out_recv.at[d], (g, frm))

    barrier = pltpu.get_barrier_semaphore()

    @pl.loop(1, n)
    def _(d):
        pl.semaphore_signal(barrier, inc=1, device_id=(g, lax.rem(f + d, n)), device_id_type=MESH)

    pl.semaphore_signal(barrier, inc=1, device_id=(partner, f), device_id_type=MESH)
    pl.semaphore_wait(barrier, n)

    w_all[f] = w_own[...]
    ring_copy(0, 0).start()
    ring_copy(1, 0).start()
    own_out = remote(w_all.at[f], w_all.at[f], own_send, own_recv, (g, sibling))
    own_out.start()

    token = lax.broadcasted_iota(jnp.int32, (tok, quads), 0) // 4
    quad = lax.broadcasted_iota(jnp.int32, (tok, quads), 1)
    frame_q = jnp.sum(jnp.where(quad <= token, starts_row[...], 0).astype(F32), axis=1, keepdims=True)
    token = lax.broadcasted_iota(jnp.int32, (quads, tok), 1) // 4
    quad = lax.broadcasted_iota(jnp.int32, (quads, tok), 0)
    frame_k = jnp.sum(jnp.where(quad <= token, starts_col[...], 0).astype(F32), axis=0, keepdims=True)
    same = frame_q == frame_k
    factor = 1.0 / math.sqrt(head)

    def attend(h):
        at = pl.ds(pl.multiple_of(h * head, head), head)
        scores = dot_nt(qkv[:, at], qkv[:, pl.ds(pl.multiple_of(width + h * head, head), head)])
        scores = jnp.where(same, scores * factor, -1e30)
        exps = jnp.exp(scores - jnp.max(scores, axis=1, keepdims=True))
        total = jnp.sum(exps, axis=1, keepdims=True)
        weights = (exps / total).astype(BF16)
        values = qkv[:, pl.ds(pl.multiple_of(2 * width + h * head, head), head)]
        ctx[:, at] = jnp.dot(weights, values, preferred_element_type=F32).astype(BF16)

    @pl.loop(0, HEADS // 5)
    def _(i):
        for u in range(5):
            attend(i * 5 + u)

    def project(j):
        acc[j] = dot_nt(ctx[...], w_all[j])

    project(f)
    remote(w_all.at[sibling], w_all.at[sibling], own_send, own_recv, (g, sibling)).wait_recv()
    project(sibling)

    def receive(side, s):
        ring_arrival(side, s).wait_recv()

        @pl.when(s + 1 < steps[side])
        def _():
            ring_copy(side, s + 1).start()

        swap_copy(side, s).start()
        core_copy(side, s).start()

    def hand_on(side, s):
        swap_arrival(side, s).wait_recv()
        core_swap_copy(side, s).start()

    def finish(side, s):
        project(ring_shard(side, s + 1))
        core_arrival(side, s).wait_recv()
        core_swap_arrival(side, s).wait_recv()
        project(core_shard(side, s + 1))

    @pl.loop(0, steps[0] + 1)
    def _(s):
        for side in range(2):

            @pl.when(s < steps[side])
            def _():
                receive(side, s)

        for act in (hand_on, finish):
            for side in range(2):

                @pl.when(jnp.logical_and(s >= 1, s <= steps[side]))
                def _():
                    act(side, s - 1)

    for j in range(n):
        at = slice(j * cols, (j + 1) * cols)
        layer_out[:, at] = (patches[:, at].astype(F32) + scale[:, at] * acc[j][:, :cols]).astype(BF16)

    row = lax.broadcasted_iota(jnp.int32, (quads, tok), 0)
    column = lax.broadcasted_iota(jnp.int32, (quads, tok), 1)
    total = jnp.zeros((quads, 1), F32)
    for q in range(4):
        pick = (column == 4 * row + q).astype(BF16)
        values = jnp.dot(pick, layer_out[...], preferred_element_type=F32)
        merged[q] = values
        total += jnp.sum(values, axis=1, keepdims=True)
    centre = total / (4 * width)
    total = jnp.zeros((quads, 1), F32)
    for q in range(4):
        centered = merged[q] - centre
        total += jnp.sum(centered * centered, axis=1, keepdims=True)
    inverse = lax.rsqrt(total / (4 * width) + 1e-05)

    row = lax.broadcasted_iota(jnp.int32, (quads, quads), 0)
    column = lax.broadcasted_iota(jnp.int32, (quads, quads), 1)
    earlier = jnp.logical_and(owners_col[...] == owners_row[...], row < column)
    ranking = jnp.sum(earlier.astype(F32), axis=0, keepdims=True).astype(jnp.int32)
    target = owners_row[...] * cap + ranking
    place_of = (lax.broadcasted_iota(jnp.int32, (n * cap, quads), 0) == target).astype(BF16)
    for q in range(4):
        normed = ((merged[q] - centre) * inverse * gain[q : q + 1] + bias[q : q + 1]).astype(BF16)
        at = slice(q * width, (q + 1) * width)
        if cap % 8 == 0:
            routed = jnp.dot(place_of, normed, preferred_element_type=F32)
            slots[:, :, at] = routed.reshape(n, cap, width).astype(BF16)
        else:
            for d in range(n):
                routed = jnp.dot(place_of[d * cap : (d + 1) * cap], normed, preferred_element_type=F32)
                slots[d, :, at] = routed.astype(BF16)

    @pl.loop(1, n)
    def _(d):
        out_copy(d).start()

    own = pltpu.make_async_copy(slots.at[f], out.at[f], local_sem)
    own.start()

    own_out.wait_send()
    for side in range(2):

        @pl.loop(0, steps[side])
        def _(s):
            ring_copy(side, s).wait_send()
            swap_copy(side, s).wait_send()
            core_copy(side, s).wait_send()
            core_swap_copy(side, s).wait_send()

    own.wait()

    @pl.loop(1, n)
    def _(d):
        out_copy(d).wait_send()
        out_arrival(d).wait_recv()


def local(mesh, qkv, patches, frame_starts, out_weight, layer_scale, norm_gain, norm_bias, owners):
    n = mesh.shape["fsdp"]
    tok, width = patches.shape
    quads = tok // 4
    cols = out_weight.shape[1]
    padded = -(-cols // 16) * 16
    part = padded // 16 // 3 * 16
    cap = max(2, 2 * quads // n)
    chips = n // 2
    w_own = jnp.pad(out_weight.T, ((0, padded - cols), (0, 0)))
    vmem = pl.BlockSpec(memory_space=pltpu.VMEM)
    sems = pltpu.SemaphoreType.DMA((2, chips // 2))
    out = pl.pallas_call(
        functools.partial(kernel, n, cols, part),
        out_shape=jax.ShapeDtypeStruct((n, cap, 4 * width), BF16),
        in_specs=[vmem] * 10,
        out_specs=pl.BlockSpec(memory_space=pl.ANY),
        scratch_shapes=[
            pltpu.VMEM((n, padded, width), BF16),
            pltpu.VMEM((tok, width), BF16),
            pltpu.VMEM((n, tok, padded), F32),
            pltpu.VMEM((tok, width), BF16),
            pltpu.VMEM((4, quads, width), F32),
            pltpu.VMEM((n, cap, 4 * width), BF16),
        ]
        + [sems] * 8
        + [
            pltpu.SemaphoreType.DMA,
            pltpu.SemaphoreType.DMA,
            pltpu.SemaphoreType.DMA((n,)),
            pltpu.SemaphoreType.DMA((n,)),
            pltpu.SemaphoreType.DMA,
        ],
        compiler_params=pltpu.CompilerParams(
            collective_id=0, has_side_effects=True, vmem_limit_bytes=60 * 1024 * 1024
        ),
    )(
        qkv,
        patches,
        frame_starts.reshape(1, quads),
        frame_starts.reshape(quads, 1),
        w_own,
        layer_scale.reshape(1, width),
        norm_gain.reshape(4, width),
        norm_bias.reshape(4, width),
        owners.reshape(1, quads),
        owners,
    )
    return out.reshape(n * cap, 4 * width)


def solution(mesh):
    return jax.shard_map(
        functools.partial(local, mesh),
        mesh=mesh,
        in_specs=(
            P(("groups", "fsdp"), None),
            P(("groups", "fsdp"), None),
            P(("groups", "fsdp")),
            P(None, "fsdp"),
            P(),
            P(),
            P(),
            P(("groups", "fsdp"), None),
        ),
        out_specs=P(("groups", "fsdp"), None),
        check_vma=False,
    )
```

time: 229 us -> 192 us (0.84)
  Pallas kernels: 0 us -> 178 us
  waiting for transfers between devices: 85.9 us -> 0 us
  blocking collectives: 77.6 us -> 0 us
  matrix products: 23.1 us -> 0 us
  between operations: 13.5 us -> 0.01 us
  local copies, waits for them, and re-layouts: 21.4 us -> 13.2 us
  other arithmetic: 5.06 us -> 0 us
    pallas_call x0 -> x1, Pallas kernels: none -> 178 us  [local(): pl.pallas_call(functools.partial(kernel, n, cols, part), out_shape=jax.Sh...]
    all_gather x1 -> x0, waiting for transfers between devices: 85.1 us -> none  [local(): full_weight = lax.all_gather(out_weight, 'fsdp', axis=1, tiled=True)]
    all_to_all x1 -> x0, blocking collectives: 77.6 us -> none  [local(): lax.all_to_all(buffer.reshape(devices, capacity, 4 * model_width), 'fsdp'...]
    dot_general x2 -> x0, matrix products: 16.5 us -> none  [the longest x1 11.7 us: local(): jnp.dot(context, full_weight, preferred_element_type=jnp.float32)]
    sub x1 -> x0, matrix products: 6.58 us -> none  [local(): exps = jnp.exp(scores - row_max)]
    slice x2 -> x0, local copies, waits for them, and re-layouts: 6.17 us -> none  [the longest x1 3.92 us: local(): qkv[:, model_width:2 * model_width].reshape(tok_rows, HEADS, head_size)]
    reshape x0 -> x4, local copies, waits for them, and re-layouts: none -> 5.55 us  [the longest x1 1.45 us: local(): norm_gain.reshape(4, width)]
    scatter x1 -> x0, local copies, waits for them, and re-layouts: 4.74 us -> none  [local(): jnp.zeros((devices * capacity, 4 * model_width), jnp.bfloat16).at[target]]
  transfers between devices with their start and end apart: 1 -> 0, of which waited for: 1 -> 0; matrix products, arithmetic and copies ran while one was open for 11% -> 0% of each run, Pallas kernels for 0% -> 0%
where the time goes in v1:
time: 192 us; the launch traced here: 191 us
  Pallas kernels  178 us (93%)
  local copies, waits for them, and re-layouts  13.2 us (7%)
    pallas_call x1, Pallas kernels, local(): pl.pallas_call(functools.partial(kernel, n, cols, part), out_shape=jax.Sh...  178 us
    unnamed x2, local copies, waits for them, and re-layouts  5.2 us

profile of v1, /device:TPU:13, one launch (start us, length us, event | category | flops | bytes accessed | tf_op | source)
XLA Modules:
  0.0 191.2 jit_solution(2882666766800336648)
XLA Ops:
  0.0 1.3 reshape.23.scale
  1.3 1.3 copy.9.starts_col
  2.7 1.4 copy.10.owners_col
  4.0 1.4 reshape.24.gain
  5.5 1.4 reshape.25.bias
  6.9 2.5 %pad.4.w_own = bf16[208,3200]{1,0:T(8,128)(2,1)} pad(bf16[200,3200]{1,0:T(8,128)(2,1)} %bitcast.6, bf16[]{:T(256)} %constant.2.clone.1), padding=0_8x0_0 | pad | bytes 2611202 | tf_op jit(solution)/shard_map/jit(_pad)/pad | solution.py:287
  9.4 178.0 %shard_map.82 = bf16[16,8,12800]{2,1,0:T(8,128)(2,1)} custom-call(bf16[256,9600]{1,0:T(8,128)(2,1)} %qkv.1, bf16[256,3200]{1,0:T(8,128)(2,1)} %patches.1, s32[1,64]{1,0:T(1,128)} %bitcast.8, s32[64,1]{1,0:T(8,128)} %copy.9.starts_col, bf16[208,3200]{1,0:T(8,128)(2,1)} %pad.4.w_own, f32[1,3200]{1,0:T(1,128)} %reshape.23.scale, f32[4,3200]{1,0:T(4,128)} %reshape.24.gain, ...), custom_call_target="tpu_custom_call" | custom-call | tf_op jit(solution)/shard_map/pallas_call | solution.py:290
  187.4 3.8 %copy.12 = bf16[128,12800]{1,0:T(8,128)(2,1)} copy(bf16[128,12800]{1,0:T(8,128)(2,1)} %bitcast.5) | data formatting | bytes 6553600

commit v2 on v1

--- a/solution.py
+++ b/solution.py
@@ -22,17 +22,20 @@
     n,
     cols,
     part,
+    qkv_hbm,
+    patches_hbm,
+    starts_row,
+    w_own,
+    scale_tiles,
+    gain_tiles,
+    bias_tiles,
+    owners_row,
+    out,
     qkv,
     patches,
-    starts_row,
-    starts_col,
-    w_own,
     scale,
     gain,
     bias,
-    owners_row,
-    owners_col,
-    out,
     w_all,
     ctx,
     acc,
@@ -52,12 +55,14 @@
     out_send,
     out_recv,
     local_sem,
+    qkv_sem,
+    patches_sem,
 ):
     tok, width = patches.shape
     head = width // HEADS
     quads = tok // 4
     cap = out.shape[1]
-    padded = w_own.shape[0]
+    padded = w_all.shape[1]
     chips = n // 2
     g = lax.axis_index("groups")
     f = lax.axis_index("fsdp")
@@ -133,6 +138,25 @@
         frm = lax.rem(f + n - d, n)
         return remote(slots.at[frm], out.at[frm], out_send.at[d], out_recv.at[d], (g, frm))
 
+    def as_column(row):
+        size = row.shape[1]
+        eye = lax.broadcasted_iota(jnp.int32, (size, size), 0) == lax.broadcasted_iota(
+            jnp.int32, (size, size), 1
+        )
+        return jnp.sum(jnp.where(eye, row.astype(F32), 0.0), axis=1, keepdims=True)
+
+    def unroll_tiles(tiles, rows):
+        per_row = width // 128
+        for q in range(rows.shape[0]):
+            for t in range(per_row):
+                at = q * per_row + t
+                rows[q : q + 1, t * 128 : (t + 1) * 128] = tiles[at : at + 1, :]
+
+    fetch_qkv = pltpu.make_async_copy(qkv_hbm, qkv, qkv_sem)
+    fetch_qkv.start()
+    fetch_patches = pltpu.make_async_copy(patches_hbm, patches, patches_sem)
+    fetch_patches.start()
+
     barrier = pltpu.get_barrier_semaphore()
 
     @pl.loop(1, n)
@@ -142,7 +166,9 @@
     pl.semaphore_signal(barrier, inc=1, device_id=(partner, f), device_id_type=MESH)
     pl.semaphore_wait(barrier, n)
 
-    w_all[f] = w_own[...]
+    w_all[f, 0:cols] = w_own[...]
+    if padded > cols:
+        w_all[f, cols:padded] = jnp.zeros((padded - cols, width), BF16)
     ring_copy(0, 0).start()
     ring_copy(1, 0).start()
     own_out = remote(w_all.at[f], w_all.at[f], own_send, own_recv, (g, sibling))
@@ -153,7 +179,7 @@
     frame_q = jnp.sum(jnp.where(quad <= token, starts_row[...], 0).astype(F32), axis=1, keepdims=True)
     token = lax.broadcasted_iota(jnp.int32, (quads, tok), 1) // 4
     quad = lax.broadcasted_iota(jnp.int32, (quads, tok), 0)
-    frame_k = jnp.sum(jnp.where(quad <= token, starts_col[...], 0).astype(F32), axis=0, keepdims=True)
+    frame_k = jnp.sum(jnp.where(quad <= token, as_column(starts_row[...]), 0.0), axis=0, keepdims=True)
     same = frame_q == frame_k
     factor = 1.0 / math.sqrt(head)
 
@@ -167,6 +193,11 @@
         values = qkv[:, pl.ds(pl.multiple_of(2 * width + h * head, head), head)]
         ctx[:, at] = jnp.dot(weights, values, preferred_element_type=F32).astype(BF16)
 
+    unroll_tiles(scale_tiles, scale)
+    unroll_tiles(gain_tiles, gain)
+    unroll_tiles(bias_tiles, bias)
+    fetch_qkv.wait()
+
     @pl.loop(0, HEADS // 5)
     def _(i):
         for u in range(5):
@@ -214,6 +245,7 @@
                 def _():
                     act(side, s - 1)
 
+    fetch_patches.wait()
     for j in range(n):
         at = slice(j * cols, (j + 1) * cols)
         layer_out[:, at] = (patches[:, at].astype(F32) + scale[:, at] * acc[j][:, :cols]).astype(BF16)
@@ -235,7 +267,7 @@
 
     row = lax.broadcasted_iota(jnp.int32, (quads, quads), 0)
     column = lax.broadcasted_iota(jnp.int32, (quads, quads), 1)
-    earlier = jnp.logical_and(owners_col[...] == owners_row[...], row < column)
+    earlier = jnp.logical_and(as_column(owners_row[...]) == owners_row[...].astype(F32), row < column)
     ranking = jnp.sum(earlier.astype(F32), axis=0, keepdims=True).astype(jnp.int32)
     target = owners_row[...] * cap + ranking
     place_of = (lax.broadcasted_iota(jnp.int32, (n * cap, quads), 0) == target).astype(BF16)
@@ -284,15 +316,19 @@
     part = padded // 16 // 3 * 16
     cap = max(2, 2 * quads // n)
     chips = n // 2
-    w_own = jnp.pad(out_weight.T, ((0, padded - cols), (0, 0)))
     vmem = pl.BlockSpec(memory_space=pltpu.VMEM)
     sems = pltpu.SemaphoreType.DMA((2, chips // 2))
     out = pl.pallas_call(
         functools.partial(kernel, n, cols, part),
         out_shape=jax.ShapeDtypeStruct((n, cap, 4 * width), BF16),
-        in_specs=[vmem] * 10,
+        in_specs=[pl.BlockSpec(memory_space=pl.ANY)] * 2 + [vmem] * 6,
         out_specs=pl.BlockSpec(memory_space=pl.ANY),
         scratch_shapes=[
+            pltpu.VMEM(qkv.shape, BF16),
+            pltpu.VMEM(patches.shape, BF16),
+            pltpu.VMEM((1, width), F32),
+            pltpu.VMEM((4, width), F32),
+            pltpu.VMEM((4, width), F32),
             pltpu.VMEM((n, padded, width), BF16),
             pltpu.VMEM((tok, width), BF16),
             pltpu.VMEM((n, tok, padded), F32),
@@ -307,6 +343,8 @@
             pltpu.SemaphoreType.DMA((n,)),
             pltpu.SemaphoreType.DMA((n,)),
             pltpu.SemaphoreType.DMA,
+            pltpu.SemaphoreType.DMA,
+            pltpu.SemaphoreType.DMA,
         ],
         compiler_params=pltpu.CompilerParams(
             collective_id=0, has_side_effects=True, vmem_limit_bytes=60 * 1024 * 1024
@@ -315,13 +353,11 @@
         qkv,
         patches,
         frame_starts.reshape(1, quads),
-        frame_starts.reshape(quads, 1),
-        w_own,
-        layer_scale.reshape(1, width),
-        norm_gain.reshape(4, width),
-        norm_bias.reshape(4, width),
+        out_weight.T,
+        layer_scale.reshape(width // 128, 128),
+        norm_gain.reshape(4 * width // 128, 128),
+        norm_bias.reshape(4 * width // 128, 128),
         owners.reshape(1, quads),
-        owners,
     )
     return out.reshape(n * cap, 4 * width)
 

time: 192 us -> 180 us (0.938)
  local copies, waits for them, and re-layouts: 13.2 us -> 3.84 us
  Pallas kernels: 178 us -> 176 us
    reshape x4 -> x0, local copies, waits for them, and re-layouts: 5.55 us -> none  [the longest x1 1.45 us: local(): norm_gain.reshape(4, width)]
    pad x1 -> x0, local copies, waits for them, and re-layouts: 2.46 us -> none  [local(): w_own = jnp.pad(out_weight.T, ((0, padded - cols), (0, 0)))]
    pallas_call x1, Pallas kernels: 178 us -> 176 us  [local(): pl.pallas_call(functools.partial(kernel, n, cols, part), out_shape=jax.Sh...]
    unnamed x2 -> x1, local copies, waits for them, and re-layouts: 5.2 us -> 3.84 us
where the time goes in v2:
time: 180 us
  Pallas kernels  176 us (98%)
  local copies, waits for them, and re-layouts  3.84 us (2%)
    pallas_call x1, Pallas kernels, local(): pl.pallas_call(functools.partial(kernel, n, cols, part), out_shape=jax.Sh...  176 us
    unnamed x1, local copies, waits for them, and re-layouts  3.84 us

profile of v2, /device:TPU:13, one launch (start us, length us, event | category | flops | bytes accessed | tf_op | source)
XLA Modules:
  0.0 179.8 jit_solution(12111639502523005673)
XLA Ops:
  0.0 175.9 %shard_map.82 = bf16[16,8,12800]{2,1,0:T(8,128)(2,1)} custom-call(bf16[256,9600]{1,0:T(8,128)(2,1)} %qkv_hbm.1, bf16[256,3200]{1,0:T(8,128)(2,1)} %patches_hbm.1, s32[1,64]{1,0:T(1,128)} %bitcast.12, bf16[200,3200]{1,0:T(8,128)(2,1)} %bitcast.8, f32[25,128]{1,0:T(8,128)} %bitcast.11, f32[100,128]{1,0:T(8,128)} %bitcast.9, f32[100,128]{1,0:T(8,128)} %bitcast.10, ...), custom_call_target="tpu_custom_call" | custom-call | tf_op jit(solution)/shard_map/pallas_call | solution.py:321
  176.0 3.8 %copy.10 = bf16[128,12800]{1,0:T(8,128)(2,1)} copy(bf16[128,12800]{1,0:T(8,128)(2,1)} %bitcast.7) | data formatting | bytes 6553600

commit v3 on v2

--- a/solution.py
+++ b/solution.py
@@ -307,6 +307,420 @@
         out_arrival(d).wait_recv()
 
 
+def overlapped_kernel(
+    n,
+    cols,
+    part,
+    qkv_hbm,
+    patches_hbm,
+    starts_row,
+    w_own,
+    scale_tiles,
+    gain_tiles,
+    bias_tiles,
+    owners_row,
+    out,
+    qkv,
+    patches,
+    scale,
+    gain,
+    bias,
+    w_all,
+    ctx,
+    acc,
+    patch_chunks,
+    scale_chunks,
+    merged,
+    slots,
+    route,
+    first_out,
+    second_out,
+    flags_out,
+    first_in,
+    second_in,
+    flags_in,
+    ring_send,
+    ring_recv,
+    swap_send,
+    swap_recv,
+    core_send,
+    core_recv,
+    core_swap_send,
+    core_swap_recv,
+    own_send,
+    own_recv,
+    first_send,
+    first_recv,
+    second_send,
+    second_recv,
+    flags_send,
+    flags_recv,
+    local_sem,
+    qkv_sem,
+    patches_sem,
+):
+    tok, width = patches.shape
+    head = width // HEADS
+    quads = tok // 4
+    cap = out.shape[0] // n
+    padded = w_all.shape[1]
+    chips = n // 2
+    g = lax.axis_index("groups")
+    f = lax.axis_index("fsdp")
+    parity = lax.rem(g, 2)
+    partner = g + 1 - 2 * parity
+    core = lax.rem(f, 2)
+    chip = f // 2
+    sibling = f + 1 - 2 * core
+    place = jnp.where(lax.rem(chip, 2) == 0, chip // 2, chips - 1 - chip // 2)
+    sign = 1 - 2 * core
+    steps = (chips // 2, chips - 1 - chips // 2)
+
+    def chip_at(p):
+        p = lax.rem(p + 2 * chips, chips)
+        return jnp.where(p < chips // 2, 2 * p, 2 * (chips - 1 - p) + 1)
+
+    def way(side):
+        return sign if side == 0 else -sign
+
+    def ring_shard(side, s):
+        return chip_at(place - way(side) * s) * 2 + core
+
+    def core_shard(side, s):
+        return chip_at(place + way(side) * s) * 2 + (1 - core)
+
+    ring_rows = pl.ds(pl.multiple_of(parity * part, 16), padded - part)
+    mine_rows = pl.ds(pl.multiple_of(parity * (padded - part), 16), part)
+    theirs_rows = pl.ds(pl.multiple_of((1 - parity) * (padded - part), 16), part)
+
+    def remote(src, dst, send, recv, device):
+        return pltpu.make_async_remote_copy(
+            src_ref=src, dst_ref=dst, send_sem=send, recv_sem=recv, device_id=device, device_id_type=MESH
+        )
+
+    def ring_copy(side, s):
+        ref = w_all.at[ring_shard(side, s), ring_rows]
+        to = chip_at(place + way(side)) * 2 + core
+        return remote(ref, ref, ring_send.at[side, s], ring_recv.at[side, s], (g, to))
+
+    def ring_arrival(side, s):
+        ref = w_all.at[ring_shard(side, s + 1), ring_rows]
+        return remote(ref, ref, ring_send.at[side, s], ring_recv.at[side, s], (g, sibling))
+
+    def swap_copy(side, s):
+        ref = w_all.at[ring_shard(side, s + 1), mine_rows]
+        return remote(ref, ref, swap_send.at[side, s], swap_recv.at[side, s], (partner, f))
+
+    def swap_arrival(side, s):
+        ref = w_all.at[ring_shard(side, s + 1), theirs_rows]
+        return remote(ref, ref, swap_send.at[side, s], swap_recv.at[side, s], (partner, f))
+
+    def core_copy(side, s):
+        ref = w_all.at[ring_shard(side, s + 1), ring_rows]
+        return remote(ref, ref, core_send.at[side, s], core_recv.at[side, s], (g, sibling))
+
+    def core_arrival(side, s):
+        ref = w_all.at[core_shard(side, s + 1), ring_rows]
+        return remote(ref, ref, core_send.at[side, s], core_recv.at[side, s], (g, sibling))
+
+    def core_swap_copy(side, s):
+        ref = w_all.at[ring_shard(side, s + 1), theirs_rows]
+        return remote(ref, ref, core_swap_send.at[side, s], core_swap_recv.at[side, s], (g, sibling))
+
+    def core_swap_arrival(side, s):
+        ref = w_all.at[core_shard(side, s + 1), theirs_rows]
+        return remote(ref, ref, core_swap_send.at[side, s], core_swap_recv.at[side, s], (g, sibling))
+
+    first = (first_out, first_in, first_send, first_recv)
+    second = (second_out, second_in, second_send, second_recv)
+    flags = (flags_out, flags_in, flags_send, flags_recv)
+
+    def out_copy(group, d):
+        source, target, send, recv = group
+        to = lax.rem(f + d, n)
+        return remote(source.at[to], target.at[f], send.at[d], recv.at[d], (g, to))
+
+    def out_arrival(group, d):
+        source, target, send, recv = group
+        frm = lax.rem(f + n - d, n)
+        return remote(source.at[frm], target.at[frm], send.at[d], recv.at[d], (g, frm))
+
+    def send_out(group):
+        source, target = group[:2]
+
+        @pl.loop(1, n)
+        def _(d):
+            out_copy(group, d).start()
+
+        target[f] = source[f]
+
+    def place_in_ring(c):
+        return c // 2 if c % 2 == 0 else chips - 1 - c // 2
+
+    def chip_of_place(p):
+        p = p % chips
+        return 2 * p if p < chips // 2 else 2 * (chips - 1 - p) + 1
+
+    mid = chips // 4
+    early = [0] + [r for s in range(1, mid + 1) for r in (s, -s)]
+    late = [r for s in range(mid + 1, chips // 2) for r in (s, -s)] + [chips // 2]
+    wide = 2 * cols
+
+    def as_column(row):
+        size = row.shape[1]
+        eye = lax.broadcasted_iota(jnp.int32, (size, size), 0) == lax.broadcasted_iota(
+            jnp.int32, (size, size), 1
+        )
+        return jnp.sum(jnp.where(eye, row.astype(F32), 0.0), axis=1, keepdims=True)
+
+    def unroll_tiles(tiles, rows):
+        per_row = width // 128
+        for q in range(rows.shape[0]):
+            for t in range(per_row):
+                at = q * per_row + t
+                rows[q : q + 1, t * 128 : (t + 1) * 128] = tiles[at : at + 1, :]
+
+    fetch_qkv = pltpu.make_async_copy(qkv_hbm, qkv, qkv_sem)
+    fetch_qkv.start()
+    fetch_patches = pltpu.make_async_copy(patches_hbm, patches, patches_sem)
+    fetch_patches.start()
+
+    barrier = pltpu.get_barrier_semaphore()
+
+    @pl.loop(1, n)
+    def _(d):
+        pl.semaphore_signal(barrier, inc=1, device_id=(g, lax.rem(f + d, n)), device_id_type=MESH)
+
+    pl.semaphore_signal(barrier, inc=1, device_id=(partner, f), device_id_type=MESH)
+    pl.semaphore_wait(barrier, n)
+
+    w_all[f, 0:cols] = w_own[...]
+    if padded > cols:
+        w_all[f, cols:padded] = jnp.zeros((padded - cols, width), BF16)
+    ring_copy(0, 0).start()
+    ring_copy(1, 0).start()
+    own_out = remote(w_all.at[f], w_all.at[f], own_send, own_recv, (g, sibling))
+    own_out.start()
+
+    token = lax.broadcasted_iota(jnp.int32, (tok, quads), 0) // 4
+    quad = lax.broadcasted_iota(jnp.int32, (tok, quads), 1)
+    frame_q = jnp.sum(jnp.where(quad <= token, starts_row[...], 0).astype(F32), axis=1, keepdims=True)
+    token = lax.broadcasted_iota(jnp.int32, (quads, tok), 1) // 4
+    quad = lax.broadcasted_iota(jnp.int32, (quads, tok), 0)
+    frame_k = jnp.sum(jnp.where(quad <= token, as_column(starts_row[...]), 0.0), axis=0, keepdims=True)
+    same = frame_q == frame_k
+    factor = 1.0 / math.sqrt(head)
+
+    def attend(h):
+        at = pl.ds(pl.multiple_of(h * head, head), head)
+        scores = dot_nt(qkv[:, at], qkv[:, pl.ds(pl.multiple_of(width + h * head, head), head)])
+        scores = jnp.where(same, scores * factor, -1e30)
+        exps = jnp.exp(scores - jnp.max(scores, axis=1, keepdims=True))
+        total = jnp.sum(exps, axis=1, keepdims=True)
+        weights = (exps / total).astype(BF16)
+        values = qkv[:, pl.ds(pl.multiple_of(2 * width + h * head, head), head)]
+        ctx[:, at] = jnp.dot(weights, values, preferred_element_type=F32).astype(BF16)
+
+    unroll_tiles(scale_tiles, scale)
+    unroll_tiles(gain_tiles, gain)
+    unroll_tiles(bias_tiles, bias)
+    fetch_qkv.wait()
+
+    @pl.loop(0, HEADS // 5)
+    def _(i):
+        for u in range(5):
+            attend(i * 5 + u)
+
+    fetch_patches.wait()
+    for c in range(chips):
+        at = slice(c * wide, (c + 1) * wide)
+        patch_chunks[c, :, :wide] = patches[:, at]
+        scale_chunks[c, :, :wide] = scale[:, at]
+
+    row = lax.broadcasted_iota(jnp.int32, (quads, quads), 0)
+    column = lax.broadcasted_iota(jnp.int32, (quads, quads), 1)
+    earlier = jnp.logical_and(as_column(owners_row[...]) == owners_row[...].astype(F32), row < column)
+    ranking = jnp.sum(earlier.astype(F32), axis=0, keepdims=True)
+    target = owners_row[...].astype(F32) * cap + ranking
+    filled = lax.broadcasted_iota(jnp.int32, (n * cap, quads), 0).astype(F32) == target
+    filled = jnp.sum(filled.astype(F32), axis=1, keepdims=True)
+    flags_out[...] = jnp.broadcast_to(filled, (n * cap, 128)).reshape(n, cap, 128)
+    token_target = jnp.sum(jnp.where(quad == token, as_column(target), 0.0), axis=0, keepdims=True)
+    row = lax.broadcasted_iota(jnp.int32, (4 * n * cap, tok), 0)
+    column = lax.broadcasted_iota(jnp.int32, (4 * n * cap, tok), 1)
+    slot = row // (4 * cap) * cap + lax.rem(row, cap)
+    part_of = lax.rem(row // cap, 4) == lax.rem(column, 4)
+    route[...] = jnp.logical_and(slot.astype(F32) == token_target, part_of).astype(BF16)
+
+    def pack(places, target):
+        for i, r in enumerate(places):
+            c = chip_at(place + r)
+            projected = jnp.concatenate([acc[2 * c][:, :cols], acc[2 * c + 1][:, :cols]], axis=1)
+            values = patch_chunks[c][:, :wide].astype(F32) + scale_chunks[c][:, :wide] * projected
+            routed = jnp.dot(route[...], values.astype(BF16), preferred_element_type=F32)
+            target[:, :, i * wide : (i + 1) * wide] = routed.reshape(n, 4 * cap, wide).astype(BF16)
+
+    def project(j):
+        acc[j] = dot_nt(ctx[...], w_all[j])
+
+    project(f)
+    remote(w_all.at[sibling], w_all.at[sibling], own_send, own_recv, (g, sibling)).wait_recv()
+    project(sibling)
+
+    def receive(side, s):
+        ring_arrival(side, s).wait_recv()
+
+        @pl.when(s + 1 < steps[side])
+        def _():
+            ring_copy(side, s + 1).start()
+
+        swap_copy(side, s).start()
+        core_copy(side, s).start()
+
+    def hand_on(side, s):
+        swap_arrival(side, s).wait_recv()
+        core_swap_copy(side, s).start()
+
+    def finish(side, s):
+        project(ring_shard(side, s + 1))
+        core_arrival(side, s).wait_recv()
+        core_swap_arrival(side, s).wait_recv()
+        project(core_shard(side, s + 1))
+
+    def turn(s):
+        for side in range(2):
+
+            @pl.when(s < steps[side])
+            def _():
+                receive(side, s)
+
+        for act in (hand_on, finish):
+            for side in range(2):
+
+                @pl.when(jnp.logical_and(s >= 1, s <= steps[side]))
+                def _():
+                    act(side, s - 1)
+
+    pl.loop(0, mid + 1)(turn)
+    pack(early, first_out)
+    send_out(first)
+    send_out(flags)
+    pl.loop(mid + 1, steps[0] + 1)(turn)
+    pack(late, second_out)
+    send_out(second)
+
+    own_out.wait_send()
+    for side in range(2):
+
+        @pl.loop(0, steps[side])
+        def _(s):
+            ring_copy(side, s).wait_send()
+            swap_copy(side, s).wait_send()
+            core_copy(side, s).wait_send()
+            core_swap_copy(side, s).wait_send()
+
+    def collect(group, places):
+        @pl.loop(1, n)
+        def _(d):
+            out_copy(group, d).wait_send()
+            out_arrival(group, d).wait_recv()
+
+        for src in range(n):
+            for i, r in enumerate(places):
+                c = chip_of_place(place_in_ring(src // 2) + r)
+                values = group[1][src, :, i * wide : (i + 1) * wide]
+                for q in range(4):
+                    merged[q, src * cap : (src + 1) * cap, c * wide : (c + 1) * wide] = values[
+                        q * cap : (q + 1) * cap
+                    ]
+
+    collect(first, early)
+    collect(flags, [])
+    collect(second, late)
+
+    def over_parts(step):
+        return lax.fori_loop(0, 4, step, jnp.zeros((n * cap, 1), F32))
+
+    def add_values(q, total):
+        return total + jnp.sum(merged[q].astype(F32), axis=1, keepdims=True)
+
+    centre = over_parts(add_values) / (4 * width)
+
+    def add_squares(q, total):
+        centered = merged[q].astype(F32) - centre
+        return total + jnp.sum(centered * centered, axis=1, keepdims=True)
+
+    inverse = lax.rsqrt(over_parts(add_squares) / (4 * width) + 1e-05)
+    present = flags_in[...].reshape(n * cap, 128)[:, :1] > 0.5
+
+    @pl.loop(0, 4)
+    def _(q):
+        values = merged[q].astype(F32)
+        normed = (values - centre) * inverse * gain[pl.ds(q, 1)] + bias[pl.ds(q, 1)]
+        normed = jnp.where(present, normed, 0.0).astype(BF16)
+        slots[:, pl.ds(pl.multiple_of(q * width, 128), width)] = normed
+
+    own = pltpu.make_async_copy(slots, out, local_sem)
+    own.start()
+    own.wait()
+
+
+def overlapped(n, cols, padded, part, cap, qkv, patches, frame_starts, out_weight, layer_scale, norm_gain, norm_bias, owners):
+    tok, width = patches.shape
+    quads = tok // 4
+    chips = n // 2
+    mid = chips // 4
+    early = -(-(2 * mid + 1) * 2 * cols // 128) * 128
+    late = -(-(chips - 2 * mid - 1) * 2 * cols // 128) * 128
+    vmem = pl.BlockSpec(memory_space=pltpu.VMEM)
+    sems = pltpu.SemaphoreType.DMA((2, chips // 2))
+    one = pltpu.SemaphoreType.DMA
+    each = pltpu.SemaphoreType.DMA((n,))
+    exchange = [
+        pltpu.VMEM((n, 4 * cap, early), BF16),
+        pltpu.VMEM((n, 4 * cap, late), BF16),
+        pltpu.VMEM((n, cap, 128), F32),
+    ]
+    return pl.pallas_call(
+        functools.partial(overlapped_kernel, n, cols, part),
+        out_shape=jax.ShapeDtypeStruct((n * cap, 4 * width), BF16),
+        in_specs=[pl.BlockSpec(memory_space=pl.ANY)] * 2 + [vmem] * 6,
+        out_specs=pl.BlockSpec(memory_space=pl.ANY),
+        scratch_shapes=[
+            pltpu.VMEM(qkv.shape, BF16),
+            pltpu.VMEM(patches.shape, BF16),
+            pltpu.VMEM((1, width), F32),
+            pltpu.VMEM((4, width), F32),
+            pltpu.VMEM((4, width), F32),
+            pltpu.VMEM((n, padded, width), BF16),
+            pltpu.VMEM((tok, width), BF16),
+            pltpu.VMEM((n, tok, padded), F32),
+            pltpu.VMEM((chips, tok, 2 * cols), BF16),
+            pltpu.VMEM((chips, 1, 2 * cols), F32),
+            pltpu.VMEM((4, n * cap, width), BF16),
+            pltpu.VMEM((n * cap, 4 * width), BF16),
+            pltpu.VMEM((4 * n * cap, tok), BF16),
+        ]
+        + exchange * 2
+        + [sems] * 8
+        + [one] * 2
+        + [each] * 6
+        + [one] * 3,
+        compiler_params=pltpu.CompilerParams(
+            collective_id=1, has_side_effects=True, vmem_limit_bytes=62 * 1024 * 1024
+        ),
+    )(
+        qkv,
+        patches,
+        frame_starts.reshape(1, quads),
+        out_weight.T,
+        layer_scale.reshape(width // 128, 128),
+        norm_gain.reshape(4 * width // 128, 128),
+        norm_bias.reshape(4 * width // 128, 128),
+        owners.reshape(1, quads),
+    )
+
+
 def local(mesh, qkv, patches, frame_starts, out_weight, layer_scale, norm_gain, norm_bias, owners):
     n = mesh.shape["fsdp"]
     tok, width = patches.shape
@@ -318,6 +732,8 @@
     chips = n // 2
     vmem = pl.BlockSpec(memory_space=pltpu.VMEM)
     sems = pltpu.SemaphoreType.DMA((2, chips // 2))
+    if cap % 8 == 0 and chips % 4 == 0:
+        return overlapped(n, cols, padded, part, cap, qkv, patches, frame_starts, out_weight, layer_scale, norm_gain, norm_bias, owners)
     out = pl.pallas_call(
         functools.partial(kernel, n, cols, part),
         out_shape=jax.ShapeDtypeStruct((n, cap, 4 * width), BF16),

time: 180 us -> 169 us (0.939)
  Pallas kernels: 176 us -> 164 us
    pallas_call x1, Pallas kernels: 176 us -> 164 us  [overlapped(): pl.pallas_call(functools.partial(overlapped_kernel, n, cols, part), out_s...]
where the time goes in v3:
time: 169 us; the launch traced here: 167 us
  Pallas kernels  164 us (97%)
  local copies, waits for them, and re-layouts  3.84 us (2%)
    pallas_call x1, Pallas kernels, overlapped(): pl.pallas_call(functools.partial(overlapped_kernel, n, cols, part), out_s...  164 us
    unnamed x1, local copies, waits for them, and re-layouts  3.84 us

profile of v3, /device:TPU:13, one launch (start us, length us, event | category | flops | bytes accessed | tf_op | source)
XLA Modules:
  0.0 167.4 jit_solution(13737245535086234700)
XLA Ops:
  0.0 163.5 %shard_map.82 = bf16[128,12800]{1,0:T(8,128)(2,1)} custom-call(bf16[256,9600]{1,0:T(8,128)(2,1)} %qkv_hbm.1, bf16[256,3200]{1,0:T(8,128)(2,1)} %patches_hbm.1, s32[1,64]{1,0:T(1,128)} %bitcast.10, bf16[200,3200]{1,0:T(8,128)(2,1)} %bitcast.6, f32[25,128]{1,0:T(8,128)} %bitcast.9, f32[100,128]{1,0:T(8,128)} %bitcast.7, f32[100,128]{1,0:T(8,128)} %bitcast.8, ...), custom_call_target="tpu_custom_call" | custom-call | tf_op jit(solution)/shard_map/pallas_call | solution.py:684
  163.5 3.8 %copy.10 = bf16[128,12800]{1,0:T(8,128)(2,1)} copy(bf16[128,12800]{1,0:T(8,128)(2,1)} %shard_map.82) | data formatting | bytes 6553600
